TPU v7x, 768 devices: a whole 4x8x12 slice. The times are simulated.
768 devices in a mesh: latent: 8 (over y_lo, core), dp: 96 (over z, y_hi, x).
Axes of the slice: x: 4, y: 8 (y_hi: 2, y_lo: 4; y = y_hi * 4 + y_lo), z: 12, core: 2. Of those that a mesh axis runs over, the one named last changes fastest.
Arguments:
- activations: bfloat16 [12288, 8192], P('dp'), may hold values from -20 to 20
- weight: float32 [768, 8192], P(('latent', 'dp')), may hold values from -2 to 2
- weight_mean: float32 [768, 8192], P(('latent', 'dp')), may hold values from -0.02 to 0.02
- weight_square: float32 [768, 8192], P(('latent', 'dp')), may hold values from 3e-05 to 0.003
- code_bias: float32 [768], P('latent'), may hold values from -3 to 3
- bias_mean: float32 [768], P('latent'), may hold values from -2 to 2
- bias_square: float32 [768], P('latent'), may hold values from 0.1 to 4
Outputs:
- after_weight: float32 [768, 8192], P(('latent', 'dp'))
- after_mean: float32 [768, 8192], P(('latent', 'dp'))
- after_square: float32 [768, 8192], P(('latent', 'dp'))
- after_bias: float32 [768], P('latent')
- after_biasmean: float32 [768], P('latent')
- after_biassquare: float32 [768], P('latent')
- total_loss: float32 [], replicated
All inputs are finite; a program needn't handle non-finite values.
Results may differ from a plain program's by a relative error of at most 0.023.
Values may be sent and summed in bfloat16 or wider, within the bound.
A program may use at most 32 MiB of HBM per device.

v0:
```python
import jax
import jax.numpy as jnp
from jax import lax
from jax.sharding import PartitionSpec as P

sparsity = 2.0
first_decay = 0.9
second_decay = 0.999
learn_rate = 0.002
adam_floor = 1e-08
first_fix = 0.9999734386011124
second_fix = 0.09520785288629108


def adam_step(value, mean, square, grad):
    mean_new = first_decay * mean + (1.0 - first_decay) * grad
    square_new = second_decay * square + (1.0 - second_decay) * grad * grad
    value_new = value - learn_rate * (mean_new / first_fix) / (
        jnp.sqrt(square_new / second_fix) + adam_floor
    )
    return (value_new, mean_new, square_new)


def per_device(activations, weight, weight_mean, weight_square, code_bias, bias_mean, bias_square):
    own_rows = weight.astype(jnp.bfloat16)
    block = lax.all_gather(own_rows, "dp", axis=0, tiled=True)
    tok_count = activations.shape[0]
    width = activations.shape[1]
    slabs = lax.axis_size("latent")
    groups = lax.axis_size("dp")
    total_tokens = tok_count * groups
    inner = (((1,), (1,)), ((), ()))
    outer = (((0,), (0,)), ((), ()))
    pre = (
        lax.dot_general(activations, block, inner, preferred_element_type=jnp.float32)
        + code_bias[None, :]
    )
    codes = jnp.maximum(pre, 0.0)
    codes_low = codes.astype(jnp.bfloat16)
    partial_value = jnp.dot(codes_low, block, preferred_element_type=jnp.float32)
    columns = width // slabs
    offset = lax.axis_index("latent") * columns
    factor = 2.0 / total_tokens
    recon = lax.psum(partial_value.astype(jnp.bfloat16), "latent").astype(jnp.float32)
    error = recon - activations.astype(jnp.float32)
    delta = (factor * error).astype(jnp.bfloat16)
    error_part = lax.dynamic_slice_in_dim(error, offset, columns, 1)
    squared = jnp.sum(error_part * error_part)
    block_wide = block.astype(jnp.float32)
    norms = jnp.sqrt(jnp.sum(block_wide * block_wide, axis=1) + 1e-06)
    penalty = jnp.sum(codes * norms[None, :])
    dcode = lax.dot_general(delta, block, inner, preferred_element_type=jnp.float32)
    dcode = dcode + sparsity / total_tokens * norms[None, :]
    dpre = jnp.where(pre > 0, dcode, 0.0)
    dpre_low = dpre.astype(jnp.bfloat16)
    counts = jnp.sum(codes, axis=0)
    grad = lax.dot_general(codes_low, delta, outer, preferred_element_type=jnp.float32)
    grad = grad + lax.dot_general(dpre_low, activations, outer, preferred_element_type=jnp.float32)
    grad = grad + (sparsity / total_tokens * counts / norms)[:, None] * block_wide
    bias_part = jnp.sum(dpre, axis=0)
    grad_own = lax.psum_scatter(grad, "dp", scatter_dimension=0, tiled=True)
    bias_grad = lax.psum(bias_part, "dp")
    squared_total, penalty_total = lax.psum((squared, penalty), ("latent", "dp"))
    total_loss = (squared_total + sparsity * penalty_total) / total_tokens
    after_weight, after_mean, after_square = adam_step(weight, weight_mean, weight_square, grad_own)
    after_bias, after_biasmean, after_biassquare = adam_step(
        code_bias, bias_mean, bias_square, bias_grad
    )
    return (
        after_weight,
        after_mean,
        after_square,
        after_bias,
        after_biasmean,
        after_biassquare,
        total_loss,
    )


def solution(mesh):
    placed = (
        P("dp", None),
        P(("latent", "dp"), None),
        P(("latent", "dp"), None),
        P(("latent", "dp"), None),
        P("latent"),
        P("latent"),
        P("latent"),
    )
    return jax.shard_map(
        per_device,
        mesh=mesh,
        in_specs=placed,
        out_specs=(
            P(("latent", "dp"), None),
            P(("latent", "dp"), None),
            P(("latent", "dp"), None),
            P("latent"),
            P("latent"),
            P("latent"),
            P(),
        ),
        check_vma=False,
    )
```

profile of v0, /device:TPU:8, one launch (start us, length us, event | category | flops | bytes accessed | tf_op | source)
XLA Modules:
  0.0 1600.0 jit_solution(8465119026887872406)
XLA Ops:
  7.2 0.0 all-gather.3.cloned.1.call-start
  7.2 1.4 convert_bitcast_fusion
  8.6 0.0 all-gather.3.cloned.1.call-update
  8.6 0.0 copy-start
  8.6 0.0 copy-start.7
  8.7 0.0 all-reduce.5.cloned.1.call-start
  8.7 204.9 %all-gather.3.cloned.1.call-done = bf16[96,1,8192]{2,1,0:T(2,128)(2,1)} async-done(((bf16[1,1,8192]{2,1,0:T(2,128)(2,1)}), bf16[96,1,8192]{2,1,0:T(2,128)(2,1)}) %all-gather.3.cloned.1.call-update) | async-done | bytes 1572880 | tf_op jit(solution)/shard_map/all_gather | solution.py:26
  213.6 4.4 fusion.1
  218.1 0.0 copy-start.1
  218.1 0.0 copy-done
  218.1 0.0 copy-done.7
  218.1 1.5 multiply_reduce_fusion.1
  219.6 0.0 copy-done.1
  219.6 2.1 convolution_convert_fusion
  221.6 0.0 all-reduce.5.cloned.1.call-update
  221.7 0.0 all-reduce.7.cloned.1.call-start
  221.7 82.4 %all-reduce.5.cloned.1.call-done = bf16[128,8192]{1,0:T(8,128)(2,1)} async-done(((bf16[128,8192]{1,0:T(8,128)(2,1)}), bf16[128,8192]{1,0:T(8,128)(2,1)}) %all-reduce.5.cloned.1.call-update) | async-done | bytes 2097168 | tf_op jit(solution)/shard_map/psum | solution.py:44
  304.1 0.0 copy-start.2
  304.1 0.0 copy-start.3
  304.1 2.7 fusion.16
  306.8 0.0 copy-done.2
  306.8 0.0 copy-done.3
  306.8 1.1 fusion.26
  308.0 2.7 fusion
  310.7 0.0 all-reduce.7.cloned.1.call-update
  310.7 1.2 dynamic-slice
  312.0 0.0 copy-start.8
  312.0 0.0 copy-start.9
  312.0 0.0 copy-start.4
  312.0 0.0 copy-start.5
  312.0 0.0 copy-start.6
  312.0 2.3 convert_subtract_fusion
  314.3 0.7 multiply_reduce_fusion
  315.1 113.1 %all-reduce.1 = (f32[]{:T(128)}, f32[]{:T(128)}) all-reduce(f32[]{:T(128)} %multiply_reduce_fusion, f32[]{:T(128)} %get-tuple-element.7), channel_id=1, replica_groups=mesh['latent'=8,'dp'=96] {'latent','dp'}, use_global_device_ids=true, to_apply=%region_7.8 | all-reduce | flops 2 | bytes 16 | tf_op jit(solution)/shard_map/psum | solution.py:63
  429.5 325.5 %psum.29 = f32[96]{0:T(128)S(1)} all-reduce(f32[96]{0:T(128)S(1)} %get-tuple-element.22), channel_id=1, replica_groups=mesh['latent'=8,'dp'=96] {'dp'}, use_global_device_ids=true, to_apply=%region_5.6 | all-reduce | flops 96 | bytes 768 | tf_op jit(solution)/shard_map/psum | solution.py:62
  755.0 0.0 copy-done.8
  755.0 0.0 copy-done.9
  755.0 0.5 divide_subtract_fusion.1
  755.5 834.4 %all-reduce.7.cloned.1.call-done = f32[96,8192]{1,0:T(8,128)} async-done(((f32[96,8192]{1,0:T(8,128)}), f32[96,8192]{1,0:T(8,128)}) %all-reduce.7.cloned.1.call-update) | async-done | bytes 3145744
  1589.9 0.0 copy-done.4
  1589.9 0.0 copy-done.5
  1589.9 0.0 copy-done.6
  1589.9 2.4 divide_subtract_fusion
  (2 shorter events, 0.0 us)
Async XLA Ops:
  7.2 206.5 %all-gather.3.cloned.1.call-start = ((), (), s32[]{:S(2)}) async-start(), calls=%async_computation.1 | async-start | bytes 3178496 | tf_op jit(solution)/shard_map/all_gather | solution.py:26
  8.6 209.5 %copy-start = (bf16[128,8192]{1,0:T(8,128)(2,1)S(1)}, bf16[128,8192]{1,0:T(8,128)(2,1)}, u32[]{:S(2)}) copy-start(bf16[128,8192]{1,0:T(8,128)(2,1)} %param.7) | copy-start | bytes 6291460
  8.6 209.5 %copy-start.7 = (f32[96]{0:T(128)S(1)}, f32[96]{0:T(128)}, u32[]{:S(2)}) copy-start(f32[96]{0:T(128)} %param.11) | copy-start | bytes 1156
  8.7 295.5 %all-reduce.5.cloned.1.call-start = ((), (), s32[]{:S(2)}) async-start(), calls=%async_computation | async-start | bytes 4194304 | tf_op jit(solution)/shard_map/psum | solution.py:44
  218.1 1.5 copy-start.1
  221.7 1368.3 %all-reduce.7.cloned.1.call-start = ((), (), s32[]{:S(2)}) async-start(), calls=%async_computation.2 | async-start | bytes 6291456
  304.1 2.7 copy-start.2
  304.1 2.7 copy-start.3
  312.0 443.0 %copy-start.8 = (f32[96]{0:T(128)S(1)}, f32[96]{0:T(128)}, u32[]{:S(2)}) copy-start(f32[96]{0:T(128)} %param.12) | copy-start | bytes 1156
  312.0 443.0 %copy-start.9 = (f32[96]{0:T(128)S(1)}, f32[96]{0:T(128)}, u32[]{:S(2)}) copy-start(f32[96]{0:T(128)} %param.13) | copy-start | bytes 1156
  312.0 1277.9 %copy-start.4 = (f32[1,8192]{1,0:T(1,128)S(1)}, f32[1,8192]{1,0:T(1,128)}, u32[]{:S(2)}) copy-start(f32[1,8192]{1,0:T(1,128)} %param.8) | copy-start | bytes 98308
  312.0 1277.9 %copy-start.5 = (f32[1,8192]{1,0:T(1,128)S(1)}, f32[1,8192]{1,0:T(1,128)}, u32[]{:S(2)}) copy-start(f32[1,8192]{1,0:T(1,128)} %param.9) | copy-start | bytes 98308
  312.0 1277.9 %copy-start.6 = (f32[1,8192]{1,0:T(1,128)S(1)}, f32[1,8192]{1,0:T(1,128)}, u32[]{:S(2)}) copy-start(f32[1,8192]{1,0:T(1,128)} %param.10) | copy-start | bytes 98308
Sparse Core Ops, SparseCore 0:
  14.0 199.6 all-gather.2
  221.8 82.2 all-reduce.4
  310.8 1279.0 all-reduce.6
where the time goes:
time: 1600 us
  waiting for transfers between devices  1120 us (70%)
  blocking collectives  439 us (27%)
  between operations  16.3 us (1%)
    unnamed x4, waiting for transfers between devices  834 us
    psum x1, blocking collectives, per_device(): bias_grad = lax.psum(bias_part, 'dp')  325 us
    all_gather x1, waiting for transfers between devices, per_device(): block = lax.all_gather(own_rows, 'dp', axis=0, tiled=True)  205 us
    psum x1, blocking collectives, per_device(): lax.psum((squared, penalty), ('latent', 'dp'))  113 us
    psum x1, waiting for transfers between devices, per_device(): lax.psum(partial_value.astype(jnp.bfloat16), 'latent').astype(jnp.float32)  82.4 us
  transfers between devices with their start and end apart: 3, of which 3 were waited for; matrix products, arithmetic and copies ran while one was open for 0% of the time, Pallas kernels for 0%

commit v1 on v0

v1 whole, which is shorter than its diff:
```python
import functools

import jax
import jax.numpy as jnp
from jax import lax
from jax.experimental import pallas as pl
from jax.experimental.pallas import tpu as pltpu
from jax.sharding import PartitionSpec as P

sparsity = 2.0
first_decay = 0.9
second_decay = 0.999
learn_rate = 0.002
adam_floor = 1e-08
first_fix = 0.9999734386011124
second_fix = 0.09520785288629108

TOKENS = 12288
MESH = pl.DeviceIdType.MESH
bf16 = jnp.bfloat16
f32 = jnp.float32


def adam_step(value, mean, square, grad):
    mean_new = first_decay * mean + (1.0 - first_decay) * grad
    square_new = second_decay * square + (1.0 - second_decay) * grad * grad
    value_new = value - learn_rate * (mean_new / first_fix) / (
        jnp.sqrt(square_new / second_fix) + adam_floor
    )
    return (value_new, mean_new, square_new)


def split3(v):
    hi = v.astype(bf16)
    rest = v - hi.astype(f32)
    mid = rest.astype(bf16)
    low = (rest - mid.astype(f32)).astype(bf16)
    return hi, mid, low


def nt(a, b):
    return lax.dot_general(a, b, (((1,), (1,)), ((), ())), preferred_element_type=f32)


def nn(a, b):
    return jnp.dot(a, b, preferred_element_type=f32)


def fold(v):
    total = v[:, 0:128]
    for i in range(1, v.shape[1] // 128):
        total = total + v[:, i * 128 : (i + 1) * 128]
    return total


def kernel(
    act, w_ref, bias_ref, grad_ref, small_ref,
    rbuf, W, DA, LT, pq, pr, C, rown, rs, rr, dq, dr, E, gs, gr, hs, hr, hown, fs, fr,
    vx, vy, vz, vc, hot,
    a_sem, own_sem,
    p0_s, p0_r, agx_s, agx_r, right_s, right_r, left_s, left_r,
    pre_s, pre_r, code_s, code_r, core_s, core_r, dc_s, dc_r, dp_s, dp_r,
    gx_s, gx_r, gz_s, gz_r, fin_s, fin_r, vx_s, vx_r, vy_s, vy_r, vz_s, vz_r, vc_s, vc_r,
):
    l = lax.axis_index("latent")
    g = lax.axis_index("dp")
    q, c = lax.div(l, 2), lax.rem(l, 2)
    x, yh, z = lax.rem(g, 4), lax.rem(lax.div(g, 4), 2), lax.div(g, 8)
    p, h = lax.div(x, 2), lax.rem(x, 2)

    def dev(q_, yh_, x_, z_, c_):
        return (q_ * 2 + c_, z_ * 8 + yh_ * 4 + x_)

    def group_peer(i):
        q_ = lax.rem(q + (i // 4), 4)
        yh_ = lax.rem(yh + (i // 2) % 2, 2)
        h_ = lax.rem(h + i % 2, 2)
        return q_, yh_, h_

    def x_peer(d):
        return dev(q, yh, lax.rem(x + d, 4), z, c)

    def q_peer(d):
        return dev(lax.rem(q + d, 4), yh, x, z, c)

    def z_peer(d):
        return dev(q, yh, x, lax.rem(z + d, 12), c)

    def y_peer(d):
        y_ = lax.rem(yh * 4 + q + d, 8)
        return dev(lax.rem(y_, 4), lax.div(y_, 4), x, z, c)

    core_peer = dev(q, yh, x, z, 1 - c)

    def remote(src, dst, s, r, to):
        return pltpu.make_async_remote_copy(
            src_ref=src, dst_ref=dst, send_sem=s, recv_sem=r, device_id=to, device_id_type=MESH
        )

    loads = [
        pltpu.make_async_copy(
            act.at[:, pl.ds(pl.multiple_of(q * 2048 + half * 1024, 1024), 1024)],
            DA.at[half, pl.ds(128, 128)],
            a_sem.at[half],
        )
        for half in range(2)
    ]
    for copy in loads:
        copy.start()

    barrier = pltpu.get_barrier_semaphore()
    count = 0
    for i in range(1, 16):
        q_, yh_, h_ = group_peer(i)
        pl.semaphore_signal(
            barrier, inc=1, device_id=dev(q_, yh_, 2 * p + h_, z, c), device_id_type=MESH
        )
        count += 1
    for d in range(1, 4):
        pl.semaphore_signal(barrier, inc=1, device_id=x_peer(d), device_id_type=MESH)
        count += 1
    for d in range(1, 12):
        pl.semaphore_signal(barrier, inc=1, device_id=z_peer(d), device_id_type=MESH)
        count += 1
    pl.semaphore_signal(barrier, inc=1, device_id=core_peer, device_id_type=MESH)
    count += 1
    pl.semaphore_wait(barrier, count)

    r_own = q * 4 + yh * 2 + h

    def piece(q_, h_):
        return w_ref.at[:, pl.ds(pl.multiple_of((q_ * 2 + h_) * 1024, 1024), 1024)]

    p0 = []
    for i in range(1, 16):
        q_, yh_, h_ = group_peer(i)
        p0.append(
            remote(
                piece(q_, h_), rbuf.at[r_own], p0_s.at[i], p0_r.at[i],
                dev(q_, yh_, 2 * p + h_, z, c),
            )
        )
    for copy in p0:
        copy.start()
    own = pltpu.make_async_copy(piece(q, h), rbuf.at[r_own], own_sem)
    own.start()

    col = lax.broadcasted_iota(jnp.int32, (96, 384), 1)
    row = lax.broadcasted_iota(jnp.int32, (96, 384), 0)
    pc = jnp.where(col >= 192, 1, 0)
    zc = (col - 192 * pc) >> 4
    rc = col & 15
    held = zc * 8 + ((rc >> 1) & 1) * 4 + pc * 2 + (rc & 1)
    hot[...] = jnp.where((held == row) & ((rc >> 2) == q), 1.0, 0.0).astype(bf16)
    bias8 = jnp.broadcast_to(bias_ref[...], (8, 96))
    bias_wide = sum(nn(part, hot[...]) for part in split3(bias8))[0:1, :]

    own.wait()
    for copy in p0:
        copy.wait_recv()
    W[h, p, z] = jnp.concatenate([rbuf[i] for i in range(16)], axis=0).astype(bf16)

    def block(j, z_):
        x_ = lax.rem(x + j, 4)
        return W.at[lax.rem(x_, 2), lax.div(x_, 2), lax.rem(z_ + 12, 12)]

    agx = [
        remote(block(0, z), block(0, z), agx_s.at[d], agx_r.at[d], x_peer(d)) for d in range(1, 4)
    ]
    for copy in agx:
        copy.start()

    def right(k, j):
        b = block(j, z - k)
        return remote(b, b, right_s.at[k, j], right_r.at[k, j], z_peer(1))

    def left(k, j):
        b = block(j, z + k)
        return remote(b, b, left_s.at[k, j], left_r.at[k, j], z_peer(11))

    def wait_right(k, j):
        b = block(j, z - k - 1)
        remote(b, b, right_s.at[k, j], right_r.at[k, j], z_peer(1)).wait_recv()

    def wait_left(k, j):
        b = block(j, z + k + 1)
        remote(b, b, left_s.at[k, j], left_r.at[k, j], z_peer(11)).wait_recv()

    for j in (0, 1, 3, 2):
        if j:
            b = block(j, z)
            remote(b, b, agx_s.at[4 - j], agx_r.at[4 - j], x_peer(4 - j)).wait_recv()
        right(0, j).start()
        left(0, j).start()

    @pl.loop(1, 5)
    def _(k):
        for j in (0, 1, 3, 2):
            wait_right(k - 1, j)
            right(k, j).start()
            wait_left(k - 1, j)
            left(k, j).start()

    for j in (0, 1, 3, 2):
        wait_right(4, j)
        right(5, j).start()
    for j in (0, 1, 3, 2):
        wait_left(4, j)
    for j in (0, 1, 3, 2):
        wait_right(5, j)

    for copy in loads:
        copy.wait()

    def rows(half):
        return W[half].reshape(384, 1024)

    pre_part = nt(DA[0, 128:256], rows(0)) + nt(DA[1, 128:256], rows(1)) + bias_wide
    pq[...] = pre_part.reshape(4, 32, 384)
    pre_send = []
    for d in (2, 1, 3):
        pre_send.append(
            remote(pq.at[lax.rem(q + d, 4)], pr.at[d], pre_s.at[d], pre_r.at[d], q_peer(d))
        )
    for copy in pre_send:
        copy.start()

    ones = jnp.ones((8, 1024), bf16)
    squares = jnp.zeros((8, 384), f32)
    for half in range(2):
        wide = rows(half).astype(f32)
        sq = wide * wide
        hi = sq.astype(bf16)
        low = (sq - hi.astype(f32)).astype(bf16)
        squares = squares + nt(ones, hi) + nt(ones, low)
    for s in range(4):
        dq[s, 32:40] = squares

    for copy in pre_send:
        copy.wait_recv()
    pre = (pq[q] + pr[1]) + (pr[2] + pr[3])
    codes = jnp.maximum(pre, 0.0)
    C[q] = codes.astype(bf16)
    code_send = [
        remote(C.at[q], C.at[q], code_s.at[d], code_r.at[d], q_peer(d)) for d in (2, 1, 3)
    ]
    for copy in code_send:
        copy.start()
    for d in (1, 3, 2):
        b = C.at[lax.rem(q + 4 - d, 4)]
        remote(b, b, code_s.at[d], code_r.at[d], q_peer(d)).wait_recv()
    codes_low = C[...].reshape(128, 384)

    core_send = []
    for half in range(2):
        part = nn(codes_low, rows(half))
        rown[half] = part
        rs[half] = part.astype(bf16)
        copy = remote(rs.at[half], rr.at[half], core_s.at[half], core_r.at[half], core_peer)
        copy.start()
        core_send.append(copy)
    codes_t = jnp.transpose(codes_low.astype(f32)).astype(bf16)
    LT[0, :, 0:128] = codes_t[0:192]
    LT[1, :, 0:128] = codes_t[192:384]
    squared = jnp.zeros((1, 128), f32)
    dcode_part = jnp.zeros((128, 384), f32)
    for half in range(2):
        core_send[half].wait_recv()
        for t in range(4):
            at = slice(t * 32, t * 32 + 32)
            error = (rown[half, at] + rr[half, at].astype(f32)) - DA[
                half, 128 + t * 32 : 160 + t * 32
            ].astype(f32)
            DA[half, at] = (error * (2.0 / TOKENS)).astype(bf16)
            squared = squared + fold(jnp.sum(error * error, axis=0, keepdims=True))
        dcode_part = dcode_part + nt(DA[half, 0:128], rows(half))
    for s in range(4):
        dq[s, 0:32] = dcode_part[s * 32 : s * 32 + 32]
    dc_send = []
    for d in (2, 1, 3):
        dc_send.append(
            remote(dq.at[lax.rem(q + d, 4)], dr.at[d], dc_s.at[d], dc_r.at[d], q_peer(d))
        )
    for copy in dc_send:
        copy.start()
    for copy in dc_send:
        copy.wait_recv()
    dcode = (dq[q] + dr[1]) + (dr[2] + dr[3])
    norms = jnp.sqrt(dcode[32:33] + 1e-6)
    dcode = dcode[0:32] + (sparsity / TOKENS) * norms
    dpre = jnp.where(pre > 0, dcode, 0.0)
    E[q] = dpre.astype(bf16)
    dp_send = [remote(E.at[q], E.at[q], dp_s.at[d], dp_r.at[d], q_peer(d)) for d in (2, 1, 3)]
    for copy in dp_send:
        copy.start()

    bias_part = jnp.sum(dpre, axis=0, keepdims=True)
    counts = jnp.sum(codes, axis=0, keepdims=True)
    loss_part = 0.5 * squared + sparsity * fold(counts * norms)
    vx[x] = jnp.concatenate(
        [bias_part[:, i * 128 : i * 128 + 128] for i in range(3)]
        + [counts[:, i * 128 : i * 128 + 128] for i in range(3)]
        + [loss_part, jnp.zeros((1, 128), f32)],
        axis=0,
    )
    vx_send = [remote(vx.at[x], vx.at[x], vx_s.at[d], vx_r.at[d], x_peer(d)) for d in range(1, 4)]
    for copy in vx_send:
        copy.start()

    for d in (1, 3, 2):
        b = E.at[lax.rem(q + 4 - d, 4)]
        remote(b, b, dp_s.at[d], dp_r.at[d], q_peer(d)).wait_recv()
    dpre_t = jnp.transpose(E[...].reshape(128, 384).astype(f32)).astype(bf16)
    LT[0, :, 128:256] = dpre_t[0:192]
    LT[1, :, 128:256] = dpre_t[192:384]

    for j in (2, 1, 3, 0):
        x_ = lax.rem(x + j, 4)
        part = nn(LT[lax.div(x_, 2)], DA[lax.rem(x_, 2)])
        gs[j] = part.astype(bf16).reshape(12, 16, 1024)

    def order(i):
        k = 6 + (1 - 2 * lax.rem(i, 2)) * lax.div(i + 1, 2)
        return k, lax.rem(z + k, 12)

    def gx(i, j):
        k, z_ = order(i)
        return remote(gs.at[j, z_], gr.at[j, z_], gx_s.at[j, i], gx_r.at[j, i], x_peer(j))

    @pl.loop(0, 12)
    def _(i):
        for j in (2, 1, 3):
            gx(i, j).start()

    for d in range(1, 4):
        b = vx.at[lax.rem(x + 4 - d, 4)]
        remote(b, b, vx_s.at[d], vx_r.at[d], x_peer(d)).wait_recv()
    y = yh * 4 + q
    vy[y] = (vx[0] + vx[1]) + (vx[2] + vx[3])
    vy_send = [remote(vy.at[y], vy.at[y], vy_s.at[d], vy_r.at[d], y_peer(d)) for d in range(1, 8)]
    for copy in vy_send:
        copy.start()

    def reduce_x(i):
        k, z_ = order(i)
        for j in (1, 3, 2):
            gx(i, j).wait_recv()
        return (gs[0, z_].astype(f32) + gr[1, z_].astype(f32)) + (
            gr[2, z_].astype(f32) + gr[3, z_].astype(f32)
        )

    def gz(k):
        return remote(hs.at[k], hr.at[k], gz_s.at[k], gz_r.at[k], z_peer(k))

    def send_z(i):
        k, _ = order(i)
        hs[k] = reduce_x(i).astype(bf16)
        gz(k).start()

    @pl.loop(0, 6)
    def _(i):
        send_z(i)

    for d in range(1, 8):
        b = vy.at[lax.rem(y + 8 - d, 8)]
        remote(b, b, vy_s.at[d], vy_r.at[d], y_peer(d)).wait_recv()
    v = vy[0]
    for i in range(1, 8):
        v = v + vy[i]
    vz[z] = v
    vz_send = [remote(vz.at[z], vz.at[z], vz_s.at[d], vz_r.at[d], z_peer(d)) for d in range(1, 12)]
    for copy in vz_send:
        copy.start()

    @pl.loop(6, 11)
    def _(i):
        send_z(i)

    hown[...] = reduce_x(11)

    for d in range(1, 12):
        b = vz.at[lax.rem(z + 12 - d, 12)]
        remote(b, b, vz_s.at[d], vz_r.at[d], z_peer(d)).wait_recv()
    v = vz[0]
    for i in range(1, 12):
        v = v + vz[i]
    vc[0] = v
    vc_send = remote(vc.at[0], vc.at[1], vc_s.at[0], vc_r.at[0], core_peer)
    vc_send.start()

    @pl.loop(0, 11)
    def _(i):
        k, _ = order(i)
        gz(k).wait_recv()
        hown[...] += hr[k].astype(f32)

    total = hown[...]
    for i in range(16):
        fs[i] = total[i : i + 1]
    slot = (q * 2 + h) * 2 + yh
    fin = []
    for i in range(1, 16):
        q_, yh_, h_ = group_peer(i)
        fin.append(
            remote(
                fs.at[q_ * 4 + yh_ * 2 + h_], fr.at[slot], fin_s.at[i], fin_r.at[i],
                dev(q_, yh_, 2 * p + h_, z, c),
            )
        )
    for copy in fin:
        copy.start()
    fr[slot] = fs[r_own]

    bias8 = jnp.concatenate([v[0:1], v[1:2], v[2:3]], axis=1)
    bias8 = jnp.broadcast_to(bias8, (8, 384))
    bias_grad = sum(nt(part, hot[...]) for part in split3(bias8))[0:1, :]
    index = p * 192 + z * 16 + r_own
    lane = lax.broadcasted_iota(jnp.int32, (1, 128), 1)
    mine = jnp.zeros((1, 128), f32)
    for i in range(3):
        mine = mine + jnp.where(lane + i * 128 == index, v[3 + i : 4 + i], 0.0)
    my_count = jnp.sum(mine, axis=1, keepdims=True)
    vc_send.wait_recv()
    loss = jnp.sum(v[6:7] + vc[1, 6:7], axis=1, keepdims=True) * (1.0 / TOKENS)
    small_ref[...] = jnp.zeros((8, 128), f32)
    small_ref[0:1, 0:96] = bias_grad
    small_ref[1:2, :] = jnp.broadcast_to(loss, (1, 128))

    own_row = w_ref[...].astype(bf16).astype(f32)
    own_norm = jnp.sqrt(jnp.sum(own_row * own_row, axis=1, keepdims=True) + 1e-6)
    scale = (sparsity / TOKENS) * my_count / own_norm
    for copy in fin:
        copy.wait_recv()
    for s in range(8):
        at = slice(s * 1024, s * 1024 + 1024)
        grad_ref[:, at] = (fr[2 * s] + fr[2 * s + 1]) + scale * own_row[:, at]

    for copy in p0 + agx + pre_send + code_send + core_send + dc_send + dp_send + fin:
        copy.wait_send()
    for copy in vx_send + vy_send + vz_send + [vc_send]:
        copy.wait_send()

    @pl.loop(0, 5)
    def _(k):
        for j in range(4):
            right(k, j).wait_send()
            left(k, j).wait_send()

    for j in range(4):
        right(5, j).wait_send()

    @pl.loop(0, 12)
    def _(i):
        for j in (1, 2, 3):
            gx(i, j).wait_send()

    @pl.loop(1, 12)
    def _(k):
        gz(k).wait_send()


def step(activations, weight, code_bias):
    dma = pltpu.SemaphoreType.DMA
    vmem = pltpu.VMEM
    return pl.pallas_call(
        kernel,
        out_shape=(
            jax.ShapeDtypeStruct((1, 8192), f32),
            jax.ShapeDtypeStruct((8, 128), f32),
        ),
        in_specs=[
            pl.BlockSpec(memory_space=pl.ANY),
            pl.BlockSpec(memory_space=pltpu.VMEM),
            pl.BlockSpec(memory_space=pltpu.VMEM),
        ],
        out_specs=[pl.BlockSpec(memory_space=pltpu.VMEM)] * 2,
        scratch_shapes=[
            vmem((16, 1, 1024), f32),
            vmem((2, 2, 12, 16, 1024), bf16),
            vmem((2, 256, 1024), bf16),
            vmem((2, 192, 256), bf16),
            vmem((4, 32, 384), f32),
            vmem((4, 32, 384), f32),
            vmem((4, 32, 384), bf16),
            vmem((2, 128, 1024), f32),
            vmem((2, 128, 1024), bf16),
            vmem((2, 128, 1024), bf16),
            vmem((4, 40, 384), f32),
            vmem((4, 40, 384), f32),
            vmem((4, 32, 384), bf16),
            vmem((4, 12, 16, 1024), bf16),
            vmem((4, 12, 16, 1024), bf16),
            vmem((12, 16, 1024), bf16),
            vmem((12, 16, 1024), bf16),
            vmem((16, 1024), f32),
            vmem((16, 1, 1024), f32),
            vmem((16, 1, 1024), f32),
            vmem((4, 8, 128), f32),
            vmem((8, 8, 128), f32),
            vmem((12, 8, 128), f32),
            vmem((2, 8, 128), f32),
            vmem((96, 384), bf16),
            dma((2,)),
            dma,
            dma((16,)), dma((16,)),
            dma((4,)), dma((4,)),
            dma((6, 4)), dma((6, 4)),
            dma((5, 4)), dma((5, 4)),
            dma((4,)), dma((4,)),
            dma((4,)), dma((4,)),
            dma((2,)), dma((2,)),
            dma((4,)), dma((4,)),
            dma((4,)), dma((4,)),
            dma((4, 12)), dma((4, 12)),
            dma((12,)), dma((12,)),
            dma((16,)), dma((16,)),
            dma((4,)), dma((4,)),
            dma((8,)), dma((8,)),
            dma((12,)), dma((12,)),
            dma((1,)), dma((1,)),
        ],
        compiler_params=pltpu.CompilerParams(
            collective_id=0, has_side_effects=True, vmem_limit_bytes=48 * 1024 * 1024
        ),
    )(activations, weight, code_bias.reshape(1, 96))


def per_device(activations, weight, weight_mean, weight_square, code_bias, bias_mean, bias_square):
    grad_own, small = step(activations, weight, code_bias)
    bias_grad = small[0, :96]
    total_loss = small[1, 0]
    after_weight, after_mean, after_square = adam_step(weight, weight_mean, weight_square, grad_own)
    after_bias, after_biasmean, after_biassquare = adam_step(
        code_bias, bias_mean, bias_square, bias_grad
    )
    return (
        after_weight,
        after_mean,
        after_square,
        after_bias,
        after_biasmean,
        after_biassquare,
        total_loss,
    )


def solution(mesh):
    placed = (
        P("dp", None),
        P(("latent", "dp"), None),
        P(("latent", "dp"), None),
        P(("latent", "dp"), None),
        P("latent"),
        P("latent"),
        P("latent"),
    )
    return jax.shard_map(
        per_device,
        mesh=mesh,
        in_specs=placed,
        out_specs=(
            P(("latent", "dp"), None),
            P(("latent", "dp"), None),
            P(("latent", "dp"), None),
            P("latent"),
            P("latent"),
            P("latent"),
            P(),
        ),
        check_vma=False,
    )
```

time: 1600 us -> 108 us (0.07)
  the two profiles are of different devices: /device:TPU:8 before, /device:TPU:1 now
where the time goes in v1:
time: 108 us; the launch traced here: 107 us
  Pallas kernels  101 us (94%)
  local copies, waits for them, and re-layouts  3.54 us (3%)
  other arithmetic  1.36 us (1%)
    pallas_call x1, Pallas kernels, step(): pl.pallas_call(kernel, out_shape=(jax.ShapeDtypeStruct((1, 8192), f32), j...  101 us
    unnamed x14, local copies, waits for them, and re-layouts  3.02 us

profile of v1, /device:TPU:1, one launch (start us, length us, event | category | flops | bytes accessed | tf_op | source)
XLA Modules:
  0.0 107.0 jit_solution(14741908068245923809)
XLA Ops:
  0.6 0.0 copy-start.6
  0.6 0.0 copy-start.5
  0.7 0.0 copy-start
  0.7 1.6 %copy-done = bf16[128,8192]{1,0:T(8,128)(2,1)S(1)} copy-done((bf16[128,8192]{1,0:T(8,128)(2,1)S(1)}, bf16[128,8192]{1,0:T(8,128)(2,1)}, u32[]{:S(2)}) %copy-start) | copy-done | bytes 2097176
  2.3 0.0 copy-start.1
  2.3 0.8 copy-done.1
  3.0 0.0 copy-start.2
  3.0 0.7 copy-done.2
  3.7 0.0 copy-start.3
  3.7 0.0 copy-start.4
  3.7 101.4 %shard_map.126 = (f32[1,8192]{1,0:T(1,128)S(1)}, f32[8,128]{1,0:T(8,128)S(1)}) custom-call(bf16[128,8192]{1,0:T(8,128)(2,1)S(1)} %copy-done, f32[1,8192]{1,0:T(1,128)S(1)} %copy-done.1, f32[1,96]{1,0:T(1,128)S(1)} %bitcast.9), custom_call_target="tpu_custom_call" | custom-call | tf_op jit(solution)/shard_map/pallas_call | solution.py:465
  105.1 0.5 slice.7
  105.6 0.0 copy-done.6
  105.6 0.0 copy-done.5
  105.6 0.5 divide_subtract_fusion.1
  106.2 0.0 copy-done.3
  106.2 0.0 copy-done.4
  106.2 0.8 divide_subtract_fusion
Async XLA Ops:
  0.6 105.0 %copy-start.6 = (f32[96]{0:T(128)S(1)}, f32[96]{0:T(128)}, u32[]{:S(2)}) copy-start(f32[96]{0:T(128)} %param.13) | copy-start | bytes 1156
  0.6 105.0 %copy-start.5 = (f32[96]{0:T(128)S(1)}, f32[96]{0:T(128)}, u32[]{:S(2)}) copy-start(f32[96]{0:T(128)} %param.12) | copy-start | bytes 1156
  0.7 1.6 %copy-start = (bf16[128,8192]{1,0:T(8,128)(2,1)S(1)}, bf16[128,8192]{1,0:T(8,128)(2,1)}, u32[]{:S(2)}) copy-start(bf16[128,8192]{1,0:T(8,128)(2,1)} %act.1) | copy-start | bytes 6291460
  2.3 0.8 copy-start.1
  3.0 0.7 copy-start.2
  3.7 102.5 %copy-start.3 = (f32[1,8192]{1,0:T(1,128)S(1)}, f32[1,8192]{1,0:T(1,128)}, u32[]{:S(2)}) copy-start(f32[1,8192]{1,0:T(1,128)} %param.9) | copy-start | bytes 98308
  3.7 102.5 %copy-start.4 = (f32[1,8192]{1,0:T(1,128)S(1)}, f32[1,8192]{1,0:T(1,128)}, u32[]{:S(2)}) copy-start(f32[1,8192]{1,0:T(1,128)} %param.10) | copy-start | bytes 98308

commit v2 on v0

v2 whole, which is shorter than its diff:
```python
import functools

import jax
import jax.numpy as jnp
from jax import lax
from jax.experimental import pallas as pl
from jax.experimental.pallas import tpu as pltpu
from jax.sharding import PartitionSpec as P

sparsity = 2.0
first_decay = 0.9
second_decay = 0.999
learn_rate = 0.002
adam_floor = 1e-08
first_fix = 0.9999734386011124
second_fix = 0.09520785288629108

TOKENS = 12288
MESH = pl.DeviceIdType.MESH
bf16 = jnp.bfloat16
f32 = jnp.float32


def adam_step(value, mean, square, grad):
    mean_new = first_decay * mean + (1.0 - first_decay) * grad
    square_new = second_decay * square + (1.0 - second_decay) * grad * grad
    value_new = value - learn_rate * (mean_new / first_fix) / (
        jnp.sqrt(square_new / second_fix) + adam_floor
    )
    return (value_new, mean_new, square_new)


def split3(v):
    hi = v.astype(bf16)
    rest = v - hi.astype(f32)
    mid = rest.astype(bf16)
    low = (rest - mid.astype(f32)).astype(bf16)
    return hi, mid, low


def nt(a, b):
    return lax.dot_general(a, b, (((1,), (1,)), ((), ())), preferred_element_type=f32)


def nn(a, b):
    return jnp.dot(a, b, preferred_element_type=f32)


def fold(v):
    total = v[:, 0:128]
    for i in range(1, v.shape[1] // 128):
        total = total + v[:, i * 128 : (i + 1) * 128]
    return total


def slot(dz):
    if dz == 6:
        return 11
    return -2 * dz - 1 if dz < 0 else 2 * dz


KINDS = ((0, 1), (1, 1), (1, 0))
CHUNKS = ((0, 8), (8, 12))


def kernel(
    act, w_any, b_any, grad_ref, small_ref,
    wv, bv, rbuf, W, DA, LT, pqa, pqb, pra, prb, ca, cb, rown, rs, rr,
    dqa, dqb, dra, drb, ea, eb, gs, gr, hs, hr, hown, fs, fr,
    vx, vy, vz, vc, hot, turn,
    a_sem, own_sem,
    p0_s, p0_r, ax_s, ax_r, ad_s, ad_r, az_s, az_r,
    pre_s, pre_r, code_s, code_r, core_s, core_r, dc_s, dc_r, dp_s, dp_r,
    gx_s, gx_r, gz_s, gz_r, fin_s, fin_r, vx_s, vx_r, vy_s, vy_r, vz_s, vz_r, vc_s, vc_r,
):
    l = lax.axis_index("latent")
    g = lax.axis_index("dp")
    q, c = lax.div(l, 2), lax.rem(l, 2)
    x, yh, z = lax.rem(g, 4), lax.rem(lax.div(g, 4), 2), lax.div(g, 8)
    p, h = lax.div(x, 2), lax.rem(x, 2)

    def dev(q_, yh_, x_, z_, c_):
        return (q_ * 2 + c_, z_ * 8 + yh_ * 4 + x_)

    def group_peer(i):
        q_ = lax.rem(q + (i // 4), 4)
        yh_ = lax.rem(yh + (i // 2) % 2, 2)
        h_ = lax.rem(h + i % 2, 2)
        return q_, yh_, h_

    def flip(bit, by):
        return 1 - bit if by else bit

    def kind_peer(kind):
        half, pair = KINDS[kind]
        return dev(q, yh, 2 * flip(p, pair) + flip(h, half), z, c)

    def x_peer(d):
        return dev(q, yh, lax.rem(x + d, 4), z, c)

    def q_peer(d):
        return dev(lax.rem(q + d, 4), yh, x, z, c)

    def z_peer(d):
        return dev(q, yh, x, lax.rem(z + d + 12, 12), c)

    def y_peer(d):
        y_ = lax.rem(yh * 4 + q + d, 8)
        return dev(lax.rem(y_, 4), lax.div(y_, 4), x, z, c)

    core_peer = dev(q, yh, x, z, 1 - c)
    started = []

    def remote(src, dst, s, r, to):
        return pltpu.make_async_remote_copy(
            src_ref=src, dst_ref=dst, send_sem=s, recv_sem=r, device_id=to, device_id_type=MESH
        )

    def start(copy):
        copy.start()
        started.append(copy.wait_send)

    barrier = pltpu.get_barrier_semaphore()
    peers = []
    for i in range(1, 16):
        q_, yh_, h_ = group_peer(i)
        peers.append(dev(q_, yh_, 2 * p + h_, z, c))
    peers += [kind_peer(0), kind_peer(1)] + [z_peer(d) for d in range(1, 12)] + [core_peer]
    for peer in peers:
        pl.semaphore_signal(barrier, inc=1, device_id=peer, device_id_type=MESH)

    loads = [
        pltpu.make_async_copy(
            act.at[:, pl.ds(pl.multiple_of(q * 2048 + flip(h, half) * 1024, 1024), 1024)],
            DA.at[half, pl.ds(128, 128)],
            a_sem.at[half],
        )
        for half in range(2)
    ]
    small_loads = [
        pltpu.make_async_copy(w_any, wv, a_sem.at[2]),
        pltpu.make_async_copy(b_any, bv, a_sem.at[3]),
    ]
    for copy in small_loads + loads:
        copy.start()

    pl.semaphore_wait(barrier, len(peers))

    r_own = q * 4 + yh * 2 + h

    def piece(q_, h_):
        return w_any.at[:, pl.ds(pl.multiple_of((q_ * 2 + h_) * 1024, 1024), 1024)]

    p0 = []
    for i in range(1, 16):
        q_, yh_, h_ = group_peer(i)
        p0.append(
            remote(
                piece(q_, h_), rbuf.at[r_own], p0_s.at[i], p0_r.at[i],
                dev(q_, yh_, 2 * p + h_, z, c),
            )
        )
    for copy in p0:
        start(copy)
    own = pltpu.make_async_copy(piece(q, h), rbuf.at[r_own], own_sem)
    own.start()

    def place(at):
        near, pair, r = at >> 5, (at >> 4) & 1, at & 15
        far = (near + 1) >> 1
        z_ = z + jnp.where((near & 1) == 1, -far, far)
        z_ = jnp.where(z_ < 0, z_ + 12, jnp.where(z_ >= 12, z_ - 12, z_))
        x_ = 2 * (p + pair - 2 * p * pair) + (r & 1)
        return (r >> 2) * 96 + z_ * 8 + ((r >> 1) & 1) * 4 + x_

    col = lax.broadcasted_iota(jnp.int32, (96, 384), 1)
    row = lax.broadcasted_iota(jnp.int32, (96, 384), 0)
    hot[...] = jnp.where(place(col) == q * 96 + row, 1.0, 0.0).astype(bf16)
    held = place(lax.broadcasted_iota(jnp.int32, (384, 128), 0))
    for i in range(3):
        to = lax.broadcasted_iota(jnp.int32, (384, 128), 1) + i * 128
        turn[:, i * 128 : i * 128 + 128] = jnp.where(held == to, 1.0, 0.0).astype(bf16)
    for copy in small_loads:
        copy.wait()
    bias8 = jnp.broadcast_to(bv[...], (8, 96))
    bias_wide = sum(nn(part, hot[...]) for part in split3(bias8))[0:1, :]
    own.wait()
    for copy in p0:
        copy.wait_recv()
    W[0, 0, 0] = jnp.concatenate([rbuf[i] for i in range(16)], axis=0).astype(bf16)

    def az(t, dz, s):
        to = slot(dz - s) if dz - s != -6 else 11
        return remote(
            W.at[0, slot(dz), t], W.at[0, to, t], az_s.at[t, to], az_r.at[t, to], z_peer(s)
        )

    def wait_z(t, dz):
        b = W.at[0, slot(dz), t]
        remote(b, b, az_s.at[t, slot(dz)], az_r.at[t, slot(dz)], z_peer(1)).wait_recv()

    def ax(kind, dz):
        at = slot(dz)
        return remote(
            W.at[0, at, 0], W.at[1, at, KINDS[kind][1]], ax_s.at[kind, at], ax_r.at[kind, at],
            kind_peer(kind),
        )

    def along_x(dz):
        start(ax(1, dz))
        start(ax(2, dz))

    def wait_x(dz):
        ax(1, dz).wait_recv()
        ax(2, dz).wait_recv()

    def onward(t, dz):
        for way in ((1, -1) if dz == 0 else (1,) if dz < 0 else (-1,)):
            for hops in (2, 1):
                if abs(dz) + hops == 6 and (dz < 0) == (t == 1):
                    continue
                start(az(t, dz, way * hops))

    two = remote(W.at[0, 0, 0], W.at[0, 0, 1], ad_s, ad_r, kind_peer(0))
    start(two)
    onward(0, 0)
    along_x(0)
    two.wait_recv()
    onward(1, 0)
    for dz in (-2, 2):
        wait_z(0, dz)
        onward(0, dz)
        along_x(dz)
    for dz in (-1, 1):
        wait_z(0, dz)
        along_x(dz)
    for dz in (-2, 2):
        wait_z(1, dz)
        onward(1, dz)
    for dz in (-4, 4):
        wait_z(0, dz)
        onward(0, dz)
        along_x(dz)
    for dz in (-3, 3):
        wait_z(0, dz)
        along_x(dz)
    for dz in (-4, 4):
        wait_z(1, dz)
        onward(1, dz)
    for copy in loads:
        copy.wait()

    def rows(half, chunk):
        first, last = CHUNKS[chunk]
        return W[half, first:last].reshape(32 * (last - first), 1024)

    def lanes(chunk):
        first, last = CHUNKS[chunk]
        return slice(32 * first, 32 * last)

    pq, pr, C = (pqa, pqb), (pra, prb), (ca, cb)
    dq, dr, E = (dqa, dqb), (dra, drb), (ea, eb)

    def to_slabs(send, recv, chunk, s, r):
        copies = [
            remote(send.at[lax.rem(q + d, 4)], recv.at[d], s.at[chunk, d], r.at[chunk, d], q_peer(d))
            for d in (2, 1, 3)
        ]
        for copy in copies:
            start(copy)
        return copies

    def share(buffer, chunk, s, r):
        for d in (2, 1, 3):
            start(
                remote(buffer.at[q], buffer.at[q], s.at[chunk, d], r.at[chunk, d], q_peer(d))
            )

    def shared(buffer, chunk, s, r):
        for d in (1, 3, 2):
            b = buffer.at[lax.rem(q + 4 - d, 4)]
            remote(b, b, s.at[chunk, d], r.at[chunk, d], q_peer(d)).wait_recv()
        return buffer[...].reshape(128, buffer.shape[2])

    def make_pre(chunk):
        part = nt(DA[0, 128:256], rows(0, chunk)) + nt(DA[1, 128:256], rows(1, chunk))
        part = part + bias_wide[:, lanes(chunk)]
        pq[chunk][...] = part.reshape(4, 32, part.shape[1])
        return to_slabs(pq[chunk], pr[chunk], chunk, pre_s, pre_r)

    def make_codes(chunk, copies):
        for copy in copies:
            copy.wait_recv()
        s, r = pq[chunk], pr[chunk]
        pre = (s[q] + r[1]) + (r[2] + r[3])
        codes = jnp.maximum(pre, 0.0)
        C[chunk][q] = codes.astype(bf16)
        share(C[chunk], chunk, code_s, code_r)
        return pre, codes

    for dz in (0, -1, 1, -2, 2, -3, 3, -4):
        wait_x(dz)
    for dz in (-1, 1, -3, 3):
        wait_z(1, dz)
    copies_a = make_pre(0)
    for dz in (-5, 5, 6):
        wait_z(0, dz)
        along_x(dz)
    for dz in (-5, 5, 6):
        wait_z(1, dz)
    for dz in (4, -5, 5, 6):
        wait_x(dz)
    copies_b = make_pre(1)
    pre_a, codes_a = make_codes(0, copies_a)

    ones = jnp.ones((8, 1024), bf16)
    for chunk in range(2):
        squares = None
        for half in range(2):
            wide = rows(half, chunk).astype(f32)
            sq = wide * wide
            hi = sq.astype(bf16)
            low = (sq - hi.astype(f32)).astype(bf16)
            part = nt(ones, hi) + nt(ones, low)
            squares = part if squares is None else squares + part
        for s in range(4):
            dq[chunk][s, 32:40] = squares

    pre_b, codes_b = make_codes(1, copies_b)
    low = [shared(C[chunk], chunk, code_s, code_r) for chunk in range(2)]

    core_send = []
    for half in range(2):
        part = nn(low[0], rows(half, 0)) + nn(low[1], rows(half, 1))
        rown[half] = part
        rs[half] = part.astype(bf16)
        copy = remote(rs.at[half], rr.at[half], core_s.at[half], core_r.at[half], core_peer)
        start(copy)
        core_send.append(copy)
    for chunk in range(2):
        LT[lanes(chunk), 0:128] = jnp.transpose(low[chunk].astype(f32)).astype(bf16)
    squared = jnp.zeros((1, 128), f32)
    for half in range(2):
        core_send[half].wait_recv()
        for t in range(4):
            at = slice(t * 32, t * 32 + 32)
            error = (rown[half, at] + rr[half, at].astype(f32)) - DA[
                half, 128 + t * 32 : 160 + t * 32
            ].astype(f32)
            DA[half, at] = (error * (2.0 / TOKENS)).astype(bf16)
            squared = squared + fold(jnp.sum(error * error, axis=0, keepdims=True))

    def make_dcode(chunk):
        part = nt(DA[0, 0:128], rows(0, chunk)) + nt(DA[1, 0:128], rows(1, chunk))
        for s in range(4):
            dq[chunk][s, 0:32] = part[s * 32 : s * 32 + 32]
        return to_slabs(dq[chunk], dr[chunk], chunk, dc_s, dc_r)

    def make_dpre(chunk, copies, pre):
        for copy in copies:
            copy.wait_recv()
        s, r = dq[chunk], dr[chunk]
        dcode = (s[q] + r[1]) + (r[2] + r[3])
        norms = jnp.sqrt(dcode[32:33] + 1e-6)
        dpre = jnp.where(pre > 0, dcode[0:32] + (sparsity / TOKENS) * norms, 0.0)
        E[chunk][q] = dpre.astype(bf16)
        share(E[chunk], chunk, dp_s, dp_r)
        return dpre, norms

    dcode_b = make_dcode(1)
    dcode_a = make_dcode(0)
    dpre_b, norms_b = make_dpre(1, dcode_b, pre_b)
    dpre_a, norms_a = make_dpre(0, dcode_a, pre_a)

    def make_grad(chunk):
        first, last = CHUNKS[chunk]
        dpre_low = shared(E[chunk], chunk, dp_s, dp_r)
        LT[lanes(chunk), 128:256] = jnp.transpose(dpre_low.astype(f32)).astype(bf16)
        for half in range(2):
            part = nn(LT[lanes(chunk)], DA[half])
            gs[half, first:last] = part.astype(bf16).reshape(last - first, 2, 16, 1024)

    def gx(at, kind):
        half, pair = KINDS[kind]
        return remote(
            gs.at[half, at, pair], gr.at[kind, at], gx_s.at[kind, at], gx_r.at[kind, at],
            kind_peer(kind),
        )

    make_grad(1)

    @pl.loop(0, 4)
    def _(i):
        for kind in range(3):
            gx(11 - i, kind).start()

    bias_part = jnp.concatenate(
        [jnp.sum(v, axis=0, keepdims=True) for v in (dpre_a, dpre_b)], axis=1
    )
    counts = jnp.concatenate(
        [jnp.sum(v, axis=0, keepdims=True) for v in (codes_a, codes_b)], axis=1
    )
    norms = jnp.concatenate([norms_a, norms_b], axis=1)
    loss_part = 0.5 * squared + sparsity * fold(counts * norms)
    both = jnp.concatenate([bias_part, counts, jnp.zeros((6, 384), f32)], axis=0)
    both = sum(nn(part, turn[...]) for part in split3(both))
    vx[x] = jnp.concatenate(
        [both[0:1, i * 128 : i * 128 + 128] for i in range(3)]
        + [both[1:2, i * 128 : i * 128 + 128] for i in range(3)]
        + [loss_part, jnp.zeros((1, 128), f32)],
        axis=0,
    )
    for d in range(1, 4):
        start(remote(vx.at[x], vx.at[x], vx_s.at[d], vx_r.at[d], x_peer(d)))

    make_grad(0)

    @pl.loop(4, 12)
    def _(i):
        for kind in range(3):
            gx(11 - i, kind).start()

    for done in started:
        done()
    started.clear()

    def x_sent():
        @pl.loop(0, 12)
        def _(i):
            for kind in range(3):
                gx(i, kind).wait_send()

    started.append(x_sent)

    for d in range(1, 4):
        b = vx.at[lax.rem(x + 4 - d, 4)]
        remote(b, b, vx_s.at[d], vx_r.at[d], x_peer(d)).wait_recv()
    y = yh * 4 + q
    vy[y] = (vx[0] + vx[1]) + (vx[2] + vx[3])
    for d in range(1, 8):
        start(remote(vy.at[y], vy.at[y], vy_s.at[d], vy_r.at[d], y_peer(d)))

    def reduce_x(at):
        for kind in (1, 2, 0):
            gx(at, kind).wait_recv()
        return (gs[0, at, 0].astype(f32) + gr[0, at].astype(f32)) + (
            gr[1, at].astype(f32) + gr[2, at].astype(f32)
        )

    def gz(at):
        far = lax.div(at + 1, 2)
        dz = (1 - 2 * lax.rem(at, 2)) * far
        return remote(hs.at[at], hr.at[at], gz_s.at[at], gz_r.at[at], z_peer(dz))

    def send_z(at):
        hs[at] = reduce_x(at).astype(bf16)
        gz(at).start()

    @pl.loop(0, 5)
    def _(i):
        send_z(11 - i)

    for d in range(1, 8):
        b = vy.at[lax.rem(y + 8 - d, 8)]
        remote(b, b, vy_s.at[d], vy_r.at[d], y_peer(d)).wait_recv()
    v = vy[0]
    for i in range(1, 8):
        v = v + vy[i]
    vz[z] = v
    for d in range(1, 12):
        start(remote(vz.at[z], vz.at[z], vz_s.at[d], vz_r.at[d], z_peer(d)))

    @pl.loop(5, 11)
    def _(i):
        send_z(11 - i)

    def z_sent():
        @pl.loop(1, 12)
        def _(k):
            gz(k).wait_send()

    started.append(z_sent)
    hown[...] = reduce_x(0)

    for d in range(1, 12):
        b = vz.at[lax.rem(z + 12 - d, 12)]
        remote(b, b, vz_s.at[d], vz_r.at[d], z_peer(d)).wait_recv()
    v = vz[0]
    for i in range(1, 12):
        v = v + vz[i]
    vc[0] = v
    vc_send = remote(vc.at[0], vc.at[1], vc_s.at[0], vc_r.at[0], core_peer)
    start(vc_send)

    @pl.loop(0, 11)
    def _(i):
        gz(11 - i).wait_recv()
        hown[...] += hr[11 - i].astype(f32)

    total = hown[...]
    for i in range(16):
        fs[i] = total[i : i + 1]
    mine = (q * 2 + h) * 2 + yh
    fin = []
    for i in range(1, 16):
        q_, yh_, h_ = group_peer(i)
        fin.append(
            remote(
                fs.at[q_ * 4 + yh_ * 2 + h_], fr.at[mine], fin_s.at[i], fin_r.at[i],
                dev(q_, yh_, 2 * p + h_, z, c),
            )
        )
    for copy in fin:
        start(copy)
    fr[mine] = fs[r_own]

    bias8 = jnp.concatenate([v[0:1], v[1:2], v[2:3]], axis=1)
    bias8 = jnp.broadcast_to(bias8, (8, 384))
    pick = jnp.where(col == q * 96 + row, 1.0, 0.0).astype(bf16)
    bias_grad = sum(nt(part, pick) for part in split3(bias8))[0:1, :]
    lane = lax.broadcasted_iota(jnp.int32, (1, 128), 1)
    own_count = jnp.zeros((1, 128), f32)
    for i in range(3):
        own_count = own_count + jnp.where(lane + i * 128 == q * 96 + g, v[3 + i : 4 + i], 0.0)
    own_count = jnp.sum(own_count, axis=1, keepdims=True)
    vc_send.wait_recv()
    loss = jnp.sum(v[6:7] + vc[1, 6:7], axis=1, keepdims=True) * (1.0 / TOKENS)
    small_ref[...] = jnp.zeros((8, 128), f32)
    small_ref[0:1, 0:96] = bias_grad
    small_ref[1:2, :] = jnp.broadcast_to(loss, (1, 128))

    for done in started[:-15]:
        done()
    own_row = wv[...].astype(bf16).astype(f32)
    own_norm = jnp.sqrt(jnp.sum(own_row * own_row, axis=1, keepdims=True) + 1e-6)
    scale = (sparsity / TOKENS) * own_count / own_norm
    for copy in fin:
        copy.wait_recv()
    for s in range(8):
        at = slice(s * 1024, s * 1024 + 1024)
        grad_ref[:, at] = (fr[2 * s] + fr[2 * s + 1]) + scale * own_row[:, at]

    for done in started[-15:]:
        done()


def step(activations, weight, code_bias):
    dma = pltpu.SemaphoreType.DMA
    vmem = pltpu.VMEM
    return pl.pallas_call(
        kernel,
        out_shape=(
            jax.ShapeDtypeStruct((1, 8192), f32),
            jax.ShapeDtypeStruct((8, 128), f32),
        ),
        in_specs=[pl.BlockSpec(memory_space=pl.ANY)] * 3,
        out_specs=[pl.BlockSpec(memory_space=pltpu.VMEM)] * 2,
        scratch_shapes=[
            vmem((1, 8192), f32),
            vmem((1, 96), f32),
            vmem((16, 1, 1024), f32),
            vmem((2, 12, 2, 16, 1024), bf16),
            vmem((2, 256, 1024), bf16),
            vmem((384, 256), bf16),
            vmem((4, 32, 256), f32), vmem((4, 32, 128), f32),
            vmem((4, 32, 256), f32), vmem((4, 32, 128), f32),
            vmem((4, 32, 256), bf16), vmem((4, 32, 128), bf16),
            vmem((2, 128, 1024), f32),
            vmem((2, 128, 1024), bf16),
            vmem((2, 128, 1024), bf16),
            vmem((4, 40, 256), f32), vmem((4, 40, 128), f32),
            vmem((4, 40, 256), f32), vmem((4, 40, 128), f32),
            vmem((4, 32, 256), bf16), vmem((4, 32, 128), bf16),
            vmem((2, 12, 2, 16, 1024), bf16),
            vmem((3, 12, 16, 1024), bf16),
            vmem((12, 16, 1024), bf16),
            vmem((12, 16, 1024), bf16),
            vmem((16, 1024), f32),
            vmem((16, 1, 1024), f32),
            vmem((16, 1, 1024), f32),
            vmem((4, 8, 128), f32),
            vmem((8, 8, 128), f32),
            vmem((12, 8, 128), f32),
            vmem((2, 8, 128), f32),
            vmem((96, 384), bf16),
            vmem((384, 384), bf16),
            dma((4,)),
            dma,
            dma((16,)), dma((16,)),
            dma((3, 12)), dma((3, 12)),
            dma, dma,
            dma((2, 12)), dma((2, 12)),
            dma((2, 4)), dma((2, 4)),
            dma((2, 4)), dma((2, 4)),
            dma((2,)), dma((2,)),
            dma((2, 4)), dma((2, 4)),
            dma((2, 4)), dma((2, 4)),
            dma((3, 12)), dma((3, 12)),
            dma((12,)), dma((12,)),
            dma((16,)), dma((16,)),
            dma((4,)), dma((4,)),
            dma((8,)), dma((8,)),
            dma((12,)), dma((12,)),
            dma((1,)), dma((1,)),
        ],
        compiler_params=pltpu.CompilerParams(
            collective_id=0, has_side_effects=True, vmem_limit_bytes=52 * 1024 * 1024
        ),
    )(activations, weight, code_bias.reshape(1, 96))


def per_device(activations, weight, weight_mean, weight_square, code_bias, bias_mean, bias_square):
    grad_own, small = step(activations, weight, code_bias)
    bias_grad = small[0, :96]
    total_loss = small[1, 0]
    after_weight, after_mean, after_square = adam_step(weight, weight_mean, weight_square, grad_own)
    after_bias, after_biasmean, after_biassquare = adam_step(
        code_bias, bias_mean, bias_square, bias_grad
    )
    return (
        after_weight,
        after_mean,
        after_square,
        after_bias,
        after_biasmean,
        after_biassquare,
        total_loss,
    )


def solution(mesh):
    placed = (
        P("dp", None),
        P(("latent", "dp"), None),
        P(("latent", "dp"), None),
        P(("latent", "dp"), None),
        P("latent"),
        P("latent"),
        P("latent"),
    )
    return jax.shard_map(
        per_device,
        mesh=mesh,
        in_specs=placed,
        out_specs=(
            P(("latent", "dp"), None),
            P(("latent", "dp"), None),
            P(("latent", "dp"), None),
            P("latent"),
            P("latent"),
            P("latent"),
            P(),
        ),
        check_vma=False,
    )
```

time: 1600 us -> 100 us (0.06)
  the two profiles are of different devices: /device:TPU:8 before, /device:TPU:1 now
where the time goes in v2:
time: 100 us; the launch traced here: 99.8 us
  Pallas kernels  95.8 us (96%)
  local copies, waits for them, and re-layouts  1.95 us (2%)
  other arithmetic  1.36 us (1%)
    pallas_call x1, Pallas kernels, step(): pl.pallas_call(kernel, out_shape=(jax.ShapeDtypeStruct((1, 8192), f32), j...  95.8 us

profile of v2, /device:TPU:1, one launch (start us, length us, event | category | flops | bytes accessed | tf_op | source)
XLA Modules:
  0.0 99.8 jit_solution(15414068731163713627)
XLA Ops:
  0.6 0.0 copy-start.5
  0.6 0.0 copy-start.4
  0.7 0.0 copy-start
  0.7 0.8 copy-done
  1.4 0.0 copy-start.1
  1.4 0.7 copy-done.1
  2.1 0.0 copy-start.2
  2.1 0.0 copy-start.3
  2.1 95.8 %shard_map.126 = (f32[1,8192]{1,0:T(1,128)S(1)}, f32[8,128]{1,0:T(8,128)S(1)}) custom-call(bf16[128,8192]{1,0:T(8,128)(2,1)} %act.1, f32[1,8192]{1,0:T(1,128)S(1)} %copy-done, f32[1,96]{1,0:T(1,128)S(1)} %bitcast.9), custom_call_target="tpu_custom_call" | custom-call | tf_op jit(solution)/shard_map/pallas_call | solution.py:550
  97.9 0.5 slice.7
  98.4 0.0 copy-done.5
  98.4 0.0 copy-done.4
  98.4 0.5 divide_subtract_fusion.1
  98.9 0.0 copy-done.2
  98.9 0.0 copy-done.3
  98.9 0.8 divide_subtract_fusion
Async XLA Ops:
  0.6 97.7 %copy-start.5 = (f32[96]{0:T(128)S(1)}, f32[96]{0:T(128)}, u32[]{:S(2)}) copy-start(f32[96]{0:T(128)} %param.13) | copy-start | bytes 1156
  0.6 97.7 %copy-start.4 = (f32[96]{0:T(128)S(1)}, f32[96]{0:T(128)}, u32[]{:S(2)}) copy-start(f32[96]{0:T(128)} %param.12) | copy-start | bytes 1156
  0.7 0.8 copy-start
  1.4 0.7 copy-start.1
  2.1 96.8 %copy-start.2 = (f32[1,8192]{1,0:T(1,128)S(1)}, f32[1,8192]{1,0:T(1,128)}, u32[]{:S(2)}) copy-start(f32[1,8192]{1,0:T(1,128)} %param.9) | copy-start | bytes 98308
  2.1 96.8 %copy-start.3 = (f32[1,8192]{1,0:T(1,128)S(1)}, f32[1,8192]{1,0:T(1,128)}, u32[]{:S(2)}) copy-start(f32[1,8192]{1,0:T(1,128)} %param.10) | copy-start | bytes 98308

commit v3 on v2

--- a/solution.py
+++ b/solution.py
@@ -214,12 +214,25 @@
         ax(1, dz).wait_recv()
         ax(2, dz).wait_recv()
 
+    STRIDE = (3, 2)
+
     def onward(t, dz):
+        if dz % STRIDE[t]:
+            return
         for way in ((1, -1) if dz == 0 else (1,) if dz < 0 else (-1,)):
-            for hops in (2, 1):
-                if abs(dz) + hops == 6 and (dz < 0) == (t == 1):
+            for hops in range(STRIDE[t], 0, -1):
+                far = abs(dz) + hops
+                if far > 6 or (far == 6 and (way == 1) == (t == 1)):
                     continue
                 start(az(t, dz, way * hops))
+
+    def pass_on(events):
+        for t, dz in events:
+            wait_z(t, dz)
+            if dz != 6:
+                onward(t, dz)
+            if t == 0:
+                along_x(dz)
 
     two = remote(W.at[0, 0, 0], W.at[0, 0, 1], ad_s, ad_r, kind_peer(0))
     start(two)
@@ -227,26 +240,7 @@
     along_x(0)
     two.wait_recv()
     onward(1, 0)
-    for dz in (-2, 2):
-        wait_z(0, dz)
-        onward(0, dz)
-        along_x(dz)
-    for dz in (-1, 1):
-        wait_z(0, dz)
-        along_x(dz)
-    for dz in (-2, 2):
-        wait_z(1, dz)
-        onward(1, dz)
-    for dz in (-4, 4):
-        wait_z(0, dz)
-        onward(0, dz)
-        along_x(dz)
-    for dz in (-3, 3):
-        wait_z(0, dz)
-        along_x(dz)
-    for dz in (-4, 4):
-        wait_z(1, dz)
-        onward(1, dz)
+    pass_on(((0, -1), (0, 1), (0, -2), (0, 2), (0, -3), (0, 3), (1, -2), (1, 2), (0, -4), (0, 4), (0, -5), (0, 5), (0, 6), (1, -4), (1, 4)))
     for copy in loads:
         copy.wait()
 
@@ -303,9 +297,7 @@
     for dz in (-1, 1, -3, 3):
         wait_z(1, dz)
     copies_a = make_pre(0)
-    for dz in (-5, 5, 6):
-        wait_z(0, dz)
-        along_x(dz)
+    pass_on(())
     for dz in (-5, 5, 6):
         wait_z(1, dz)
     for dz in (4, -5, 5, 6):
@@ -449,11 +441,17 @@
 
     def gz(at):
         far = lax.div(at + 1, 2)
-        dz = (1 - 2 * lax.rem(at, 2)) * far
-        return remote(hs.at[at], hr.at[at], gz_s.at[at], gz_r.at[at], z_peer(dz))
-
-    def send_z(at):
-        hs[at] = reduce_x(at).astype(bf16)
+        far = far - jnp.where(far > 3, 3, 0)
+        sign = 1 - 2 * lax.rem(at, 2)
+        sign = jnp.where(at == 11, 1, sign)
+        return remote(hs.at[at], hr.at[at], gz_s.at[at], gz_r.at[at], z_peer(sign * far))
+
+    def send_z(at, more=()):
+        part = reduce_x(at)
+        for other in more:
+            gz(other).wait_recv()
+            part = part + hr[other].astype(f32)
+        hs[at] = part.astype(bf16)
         gz(at).start()
 
     @pl.loop(0, 5)
@@ -470,7 +468,10 @@
     for d in range(1, 12):
         start(remote(vz.at[z], vz.at[z], vz_s.at[d], vz_r.at[d], z_peer(d)))
 
-    @pl.loop(5, 11)
+    send_z(6, (8, 10, 11))
+    send_z(5, (7, 9))
+
+    @pl.loop(7, 11)
     def _(i):
         send_z(11 - i)
 
@@ -492,10 +493,10 @@
     vc_send = remote(vc.at[0], vc.at[1], vc_s.at[0], vc_r.at[0], core_peer)
     start(vc_send)
 
-    @pl.loop(0, 11)
+    @pl.loop(0, 6)
     def _(i):
-        gz(11 - i).wait_recv()
-        hown[...] += hr[11 - i].astype(f32)
+        gz(6 - i).wait_recv()
+        hown[...] += hr[6 - i].astype(f32)
 
     total = hown[...]
     for i in range(16):

time: 100 us -> 94.5 us (0.945); the launches traced: 99.8 us -> 93.2 us
  Pallas kernels: 95.8 us -> 89.2 us
    pallas_call x1, Pallas kernels: 95.8 us -> 89.2 us  [step(): pl.pallas_call(kernel, out_shape=(jax.ShapeDtypeStruct((1, 8192), f32), j...]
where the time goes in v3:
time: 94.5 us; the launch traced here: 93.2 us
  Pallas kernels  89.2 us (94%)
  local copies, waits for them, and re-layouts  1.95 us (2%)
  other arithmetic  1.36 us (1%)
    pallas_call x1, Pallas kernels, step(): pl.pallas_call(kernel, out_shape=(jax.ShapeDtypeStruct((1, 8192), f32), j...  89.2 us

profile of v3, /device:TPU:1, one launch (start us, length us, event | category | flops | bytes accessed | tf_op | source)
XLA Modules:
  0.0 93.2 jit_solution(17378498471296499856)
XLA Ops:
  0.6 0.0 copy-start.5
  0.6 0.0 copy-start.4
  0.7 0.0 copy-start
  0.7 0.8 copy-done
  1.4 0.0 copy-start.1
  1.4 0.7 copy-done.1
  2.1 0.0 copy-start.2
  2.1 0.0 copy-start.3
  2.1 89.2 %shard_map.126 = (f32[1,8192]{1,0:T(1,128)S(1)}, f32[8,128]{1,0:T(8,128)S(1)}) custom-call(bf16[128,8192]{1,0:T(8,128)(2,1)} %act.1, f32[1,8192]{1,0:T(1,128)S(1)} %copy-done, f32[1,96]{1,0:T(1,128)S(1)} %bitcast.9), custom_call_target="tpu_custom_call" | custom-call | tf_op jit(solution)/shard_map/pallas_call | solution.py:551
  91.3 0.5 slice.7
  91.8 0.0 copy-done.5
  91.8 0.0 copy-done.4
  91.8 0.5 divide_subtract_fusion.1
  92.3 0.0 copy-done.2
  92.3 0.0 copy-done.3
  92.3 0.8 divide_subtract_fusion
Async XLA Ops:
  0.6 91.2 %copy-start.5 = (f32[96]{0:T(128)S(1)}, f32[96]{0:T(128)}, u32[]{:S(2)}) copy-start(f32[96]{0:T(128)} %param.13) | copy-start | bytes 1156
  0.6 91.2 %copy-start.4 = (f32[96]{0:T(128)S(1)}, f32[96]{0:T(128)}, u32[]{:S(2)}) copy-start(f32[96]{0:T(128)} %param.12) | copy-start | bytes 1156
  0.7 0.8 copy-start
  1.4 0.7 copy-start.1
  2.1 90.3 %copy-start.2 = (f32[1,8192]{1,0:T(1,128)S(1)}, f32[1,8192]{1,0:T(1,128)}, u32[]{:S(2)}) copy-start(f32[1,8192]{1,0:T(1,128)} %param.9) | copy-start | bytes 98308
  2.1 90.3 %copy-start.3 = (f32[1,8192]{1,0:T(1,128)S(1)}, f32[1,8192]{1,0:T(1,128)}, u32[]{:S(2)}) copy-start(f32[1,8192]{1,0:T(1,128)} %param.10) | copy-start | bytes 98308

commit v4 on v3

--- a/solution.py
+++ b/solution.py
@@ -61,6 +61,7 @@
 
 KINDS = ((0, 1), (1, 1), (1, 0))
 CHUNKS = ((0, 8), (8, 12))
+FIRST = (3, 11, 7, 15, 2, 10, 6, 14, 9, 5, 13, 8, 4, 12, 1)
 
 
 def kernel(
@@ -122,7 +123,7 @@
 
     barrier = pltpu.get_barrier_semaphore()
     peers = []
-    for i in range(1, 16):
+    for i in FIRST:
         q_, yh_, h_ = group_peer(i)
         peers.append(dev(q_, yh_, 2 * p + h_, z, c))
     peers += [kind_peer(0), kind_peer(1)] + [z_peer(d) for d in range(1, 12)] + [core_peer]
@@ -152,7 +153,7 @@
         return w_any.at[:, pl.ds(pl.multiple_of((q_ * 2 + h_) * 1024, 1024), 1024)]
 
     p0 = []
-    for i in range(1, 16):
+    for i in FIRST:
         q_, yh_, h_ = group_peer(i)
         p0.append(
             remote(
@@ -201,12 +202,17 @@
 
     def ax(kind, dz):
         at = slot(dz)
+        half, pair = KINDS[kind]
         return remote(
-            W.at[0, at, 0], W.at[1, at, KINDS[kind][1]], ax_s.at[kind, at], ax_r.at[kind, at],
+            W.at[0, at, 0], W.at[half, at, pair], ax_s.at[kind, at], ax_r.at[kind, at],
             kind_peer(kind),
         )
 
+    FAR = (-5, 5, 6)
+
     def along_x(dz):
+        if dz in FAR:
+            start(ax(0, dz))
         start(ax(1, dz))
         start(ax(2, dz))
 
@@ -222,7 +228,7 @@
         for way in ((1, -1) if dz == 0 else (1,) if dz < 0 else (-1,)):
             for hops in range(STRIDE[t], 0, -1):
                 far = abs(dz) + hops
-                if far > 6 or (far == 6 and (way == 1) == (t == 1)):
+                if far > (6, 4)[t] or (far == 6 and way == -1):
                     continue
                 start(az(t, dz, way * hops))
 
@@ -240,7 +246,7 @@
     along_x(0)
     two.wait_recv()
     onward(1, 0)
-    pass_on(((0, -1), (0, 1), (0, -2), (0, 2), (0, -3), (0, 3), (1, -2), (1, 2), (0, -4), (0, 4), (0, -5), (0, 5), (0, 6), (1, -4), (1, 4)))
+    pass_on(((0, -1), (0, 1), (0, -2), (0, 2), (0, -3), (0, 3), (1, -2), (1, 2), (0, -4), (0, 4), (0, -5), (0, 5), (0, 6)))
     for copy in loads:
         copy.wait()
 
@@ -294,12 +300,12 @@
 
     for dz in (0, -1, 1, -2, 2, -3, 3, -4):
         wait_x(dz)
-    for dz in (-1, 1, -3, 3):
+    for dz in (-1, 1, -3, 3, -4):
         wait_z(1, dz)
     copies_a = make_pre(0)
-    pass_on(())
-    for dz in (-5, 5, 6):
-        wait_z(1, dz)
+    wait_z(1, 4)
+    for dz in FAR:
+        ax(0, dz).wait_recv()
     for dz in (4, -5, 5, 6):
         wait_x(dz)
     copies_b = make_pre(1)
@@ -323,24 +329,34 @@
 
     core_send = []
     for half in range(2):
-        part = nn(low[0], rows(half, 0)) + nn(low[1], rows(half, 1))
-        rown[half] = part
-        rs[half] = part.astype(bf16)
-        copy = remote(rs.at[half], rr.at[half], core_s.at[half], core_r.at[half], core_peer)
-        start(copy)
-        core_send.append(copy)
+        for part_at in range(2):
+            cols = slice(part_at * 512, part_at * 512 + 512)
+            part = nn(low[0], W[half, 0:8, :, :, cols].reshape(256, 512)) + nn(
+                low[1], W[half, 8:12, :, :, cols].reshape(128, 512)
+            )
+            rown[half, :, cols] = part
+            rs[half, :, cols] = part.astype(bf16)
+            i = 2 * half + part_at
+            lane = pl.ds(part_at * 512, 512)
+            copy = remote(
+                rs.at[half, :, lane], rr.at[half, :, lane], core_s.at[i], core_r.at[i], core_peer
+            )
+            start(copy)
+            core_send.append(copy)
     for chunk in range(2):
         LT[lanes(chunk), 0:128] = jnp.transpose(low[chunk].astype(f32)).astype(bf16)
     squared = jnp.zeros((1, 128), f32)
     for half in range(2):
-        core_send[half].wait_recv()
-        for t in range(4):
-            at = slice(t * 32, t * 32 + 32)
-            error = (rown[half, at] + rr[half, at].astype(f32)) - DA[
-                half, 128 + t * 32 : 160 + t * 32
-            ].astype(f32)
-            DA[half, at] = (error * (2.0 / TOKENS)).astype(bf16)
-            squared = squared + fold(jnp.sum(error * error, axis=0, keepdims=True))
+        for part_at in range(2):
+            cols = slice(part_at * 512, part_at * 512 + 512)
+            core_send[2 * half + part_at].wait_recv()
+            for t in range(4):
+                at = slice(t * 32, t * 32 + 32)
+                error = (rown[half, at, cols] + rr[half, at, cols].astype(f32)) - DA[
+                    half, 128 + t * 32 : 160 + t * 32, cols
+                ].astype(f32)
+                DA[half, at, cols] = (error * (2.0 / TOKENS)).astype(bf16)
+                squared = squared + fold(jnp.sum(error * error, axis=0, keepdims=True))
 
     def make_dcode(chunk):
         part = nt(DA[0, 0:128], rows(0, chunk)) + nt(DA[1, 0:128], rows(1, chunk))
@@ -396,14 +412,15 @@
     loss_part = 0.5 * squared + sparsity * fold(counts * norms)
     both = jnp.concatenate([bias_part, counts, jnp.zeros((6, 384), f32)], axis=0)
     both = sum(nn(part, turn[...]) for part in split3(both))
-    vx[x] = jnp.concatenate(
+    y = yh * 4 + q
+    vy[y] = jnp.concatenate(
         [both[0:1, i * 128 : i * 128 + 128] for i in range(3)]
         + [both[1:2, i * 128 : i * 128 + 128] for i in range(3)]
         + [loss_part, jnp.zeros((1, 128), f32)],
         axis=0,
     )
-    for d in range(1, 4):
-        start(remote(vx.at[x], vx.at[x], vx_s.at[d], vx_r.at[d], x_peer(d)))
+    for d in range(1, 8):
+        start(remote(vy.at[y], vy.at[y], vy_s.at[d], vy_r.at[d], y_peer(d)))
 
     make_grad(0)
 
@@ -423,40 +440,6 @@
                 gx(i, kind).wait_send()
 
     started.append(x_sent)
-
-    for d in range(1, 4):
-        b = vx.at[lax.rem(x + 4 - d, 4)]
-        remote(b, b, vx_s.at[d], vx_r.at[d], x_peer(d)).wait_recv()
-    y = yh * 4 + q
-    vy[y] = (vx[0] + vx[1]) + (vx[2] + vx[3])
-    for d in range(1, 8):
-        start(remote(vy.at[y], vy.at[y], vy_s.at[d], vy_r.at[d], y_peer(d)))
-
-    def reduce_x(at):
-        for kind in (1, 2, 0):
-            gx(at, kind).wait_recv()
-        return (gs[0, at, 0].astype(f32) + gr[0, at].astype(f32)) + (
-            gr[1, at].astype(f32) + gr[2, at].astype(f32)
-        )
-
-    def gz(at):
-        far = lax.div(at + 1, 2)
-        far = far - jnp.where(far > 3, 3, 0)
-        sign = 1 - 2 * lax.rem(at, 2)
-        sign = jnp.where(at == 11, 1, sign)
-        return remote(hs.at[at], hr.at[at], gz_s.at[at], gz_r.at[at], z_peer(sign * far))
-
-    def send_z(at, more=()):
-        part = reduce_x(at)
-        for other in more:
-            gz(other).wait_recv()
-            part = part + hr[other].astype(f32)
-        hs[at] = part.astype(bf16)
-        gz(at).start()
-
-    @pl.loop(0, 5)
-    def _(i):
-        send_z(11 - i)
 
     for d in range(1, 8):
         b = vy.at[lax.rem(y + 8 - d, 8)]
@@ -468,20 +451,31 @@
     for d in range(1, 12):
         start(remote(vz.at[z], vz.at[z], vz_s.at[d], vz_r.at[d], z_peer(d)))
 
-    send_z(6, (8, 10, 11))
-    send_z(5, (7, 9))
-
-    @pl.loop(7, 11)
+    def reduce_x(at):
+        for kind in (1, 2, 0):
+            gx(at, kind).wait_recv()
+        return (gs[0, at, 0].astype(f32) + gr[0, at].astype(f32)) + (
+            gr[1, at].astype(f32) + gr[2, at].astype(f32)
+        )
+
+    def gz(at):
+        far = lax.div(at + 1, 2)
+        far = far - jnp.where(far > 3, 3, 0)
+        sign = 1 - 2 * lax.rem(at, 2)
+        sign = jnp.where(at == 11, 1, sign)
+        return remote(hs.at[at], hr.at[at], gz_s.at[at], gz_r.at[at], z_peer(sign * far))
+
+    def send_z(at, more=()):
+        part = reduce_x(at)
+        for other in more:
+            gz(other).wait_recv()
+            part = part + hr[other].astype(f32)
+        hs[at] = part.astype(bf16)
+        gz(at).start()
+
+    @pl.loop(0, 5)
     def _(i):
         send_z(11 - i)
-
-    def z_sent():
-        @pl.loop(1, 12)
-        def _(k):
-            gz(k).wait_send()
-
-    started.append(z_sent)
-    hown[...] = reduce_x(0)
 
     for d in range(1, 12):
         b = vz.at[lax.rem(z + 12 - d, 12)]
@@ -489,6 +483,29 @@
     v = vz[0]
     for i in range(1, 12):
         v = v + vz[i]
+    vx[x] = v
+    for d in range(1, 4):
+        start(remote(vx.at[x], vx.at[x], vx_s.at[d], vx_r.at[d], x_peer(d)))
+
+    send_z(6, (8, 10, 11))
+    send_z(5, (7, 9))
+
+    @pl.loop(7, 11)
+    def _(i):
+        send_z(11 - i)
+
+    def z_sent():
+        @pl.loop(1, 12)
+        def _(k):
+            gz(k).wait_send()
+
+    started.append(z_sent)
+    hown[...] = reduce_x(0)
+
+    for d in range(1, 4):
+        b = vx.at[lax.rem(x + 4 - d, 4)]
+        remote(b, b, vx_s.at[d], vx_r.at[d], x_peer(d)).wait_recv()
+    v = (vx[0] + vx[1]) + (vx[2] + vx[3])
     vc[0] = v
     vc_send = remote(vc.at[0], vc.at[1], vc_s.at[0], vc_r.at[0], core_peer)
     start(vc_send)
@@ -503,7 +520,7 @@
         fs[i] = total[i : i + 1]
     mine = (q * 2 + h) * 2 + yh
     fin = []
-    for i in range(1, 16):
+    for i in FIRST:
         q_, yh_, h_ = group_peer(i)
         fin.append(
             remote(
@@ -593,7 +610,7 @@
             dma((2, 12)), dma((2, 12)),
             dma((2, 4)), dma((2, 4)),
             dma((2, 4)), dma((2, 4)),
-            dma((2,)), dma((2,)),
+            dma((4,)), dma((4,)),
             dma((2, 4)), dma((2, 4)),
             dma((2, 4)), dma((2, 4)),
             dma((3, 12)), dma((3, 12)),

time: 94.5 us -> 94.2 us (level)
  no operation moved by 1% of the time
where the time goes in v4:
time: 94.2 us; the launch traced here: 92.5 us
  Pallas kernels  88.6 us (94%)
  local copies, waits for them, and re-layouts  1.95 us (2%)
  other arithmetic  1.36 us (1%)
    pallas_call x1, Pallas kernels, step(): pl.pallas_call(kernel, out_shape=(jax.ShapeDtypeStruct((1, 8192), f32), j...  88.6 us

profile of v4, /device:TPU:1, one launch (start us, length us, event | category | flops | bytes accessed | tf_op | source)
XLA Modules:
  0.0 92.5 jit_solution(8205890540584482924)
XLA Ops:
  0.6 0.0 copy-start.5
  0.6 0.0 copy-start.4
  0.7 0.0 copy-start
  0.7 0.8 copy-done
  1.4 0.0 copy-start.1
  1.4 0.7 copy-done.1
  2.1 0.0 copy-start.2
  2.1 0.0 copy-start.3
  2.1 88.6 %shard_map.126 = (f32[1,8192]{1,0:T(1,128)S(1)}, f32[8,128]{1,0:T(8,128)S(1)}) custom-call(bf16[128,8192]{1,0:T(8,128)(2,1)} %act.1, f32[1,8192]{1,0:T(1,128)S(1)} %copy-done, f32[1,96]{1,0:T(1,128)S(1)} %bitcast.9), custom_call_target="tpu_custom_call" | custom-call | tf_op jit(solution)/shard_map/pallas_call | solution.py:568
  90.7 0.5 slice.7
  91.2 0.0 copy-done.5
  91.2 0.0 copy-done.4
  91.2 0.5 divide_subtract_fusion.1
  91.7 0.0 copy-done.2
  91.7 0.0 copy-done.3
  91.7 0.8 divide_subtract_fusion
Async XLA Ops:
  0.6 90.5 %copy-start.5 = (f32[96]{0:T(128)S(1)}, f32[96]{0:T(128)}, u32[]{:S(2)}) copy-start(f32[96]{0:T(128)} %param.13) | copy-start | bytes 1156
  0.6 90.5 %copy-start.4 = (f32[96]{0:T(128)S(1)}, f32[96]{0:T(128)}, u32[]{:S(2)}) copy-start(f32[96]{0:T(128)} %param.12) | copy-start | bytes 1156
  0.7 0.8 copy-start
  1.4 0.7 copy-start.1
  2.1 89.6 %copy-start.2 = (f32[1,8192]{1,0:T(1,128)S(1)}, f32[1,8192]{1,0:T(1,128)}, u32[]{:S(2)}) copy-start(f32[1,8192]{1,0:T(1,128)} %param.9) | copy-start | bytes 98308
  2.1 89.6 %copy-start.3 = (f32[1,8192]{1,0:T(1,128)S(1)}, f32[1,8192]{1,0:T(1,128)}, u32[]{:S(2)}) copy-start(f32[1,8192]{1,0:T(1,128)} %param.10) | copy-start | bytes 98308

commit v5 on v4

--- a/solution.py
+++ b/solution.py
@@ -67,11 +67,11 @@
 def kernel(
     act, w_any, b_any, grad_ref, small_ref,
     wv, bv, rbuf, W, DA, LT, pqa, pqb, pra, prb, ca, cb, rown, rs, rr,
-    dqa, dqb, dra, drb, ea, eb, gs, gr, hs, hr, hown, fs, fr,
+    dqa, dqb, dra, drb, nrm, ea, eb, gs, gr, hs, hr, hown, fs, fr,
     vx, vy, vz, vc, hot, turn,
     a_sem, own_sem,
     p0_s, p0_r, ax_s, ax_r, ad_s, ad_r, az_s, az_r,
-    pre_s, pre_r, code_s, code_r, core_s, core_r, dc_s, dc_r, dp_s, dp_r,
+    pre_s, pre_r, code_s, code_r, core_s, core_r, dc_s, dc_r, nm_s, nm_r, dp_s, dp_r,
     gx_s, gx_r, gz_s, gz_r, fin_s, fin_r, vx_s, vx_r, vy_s, vy_r, vz_s, vz_r, vc_s, vc_r,
 ):
     l = lax.axis_index("latent")
@@ -321,8 +321,9 @@
             low = (sq - hi.astype(f32)).astype(bf16)
             part = nt(ones, hi) + nt(ones, low)
             squares = part if squares is None else squares + part
-        for s in range(4):
-            dq[chunk][s, 32:40] = squares
+        nrm[q, :, lanes(chunk)] = squares
+    for d in (2, 1, 3):
+        start(remote(nrm.at[q], nrm.at[q], nm_s.at[d], nm_r.at[d], q_peer(d)))
 
     pre_b, codes_b = make_codes(1, copies_b)
     low = [shared(C[chunk], chunk, code_s, code_r) for chunk in range(2)]
@@ -360,23 +361,26 @@
 
     def make_dcode(chunk):
         part = nt(DA[0, 0:128], rows(0, chunk)) + nt(DA[1, 0:128], rows(1, chunk))
-        for s in range(4):
-            dq[chunk][s, 0:32] = part[s * 32 : s * 32 + 32]
+        dq[chunk][...] = part.astype(bf16).reshape(4, 32, part.shape[1])
         return to_slabs(dq[chunk], dr[chunk], chunk, dc_s, dc_r)
 
     def make_dpre(chunk, copies, pre):
         for copy in copies:
             copy.wait_recv()
         s, r = dq[chunk], dr[chunk]
-        dcode = (s[q] + r[1]) + (r[2] + r[3])
-        norms = jnp.sqrt(dcode[32:33] + 1e-6)
-        dpre = jnp.where(pre > 0, dcode[0:32] + (sparsity / TOKENS) * norms, 0.0)
+        dcode = (s[q].astype(f32) + r[1].astype(f32)) + (r[2].astype(f32) + r[3].astype(f32))
+        norms = norms_all[:, lanes(chunk)]
+        dpre = jnp.where(pre > 0, dcode + (sparsity / TOKENS) * norms, 0.0)
         E[chunk][q] = dpre.astype(bf16)
         share(E[chunk], chunk, dp_s, dp_r)
         return dpre, norms
 
     dcode_b = make_dcode(1)
     dcode_a = make_dcode(0)
+    for d in (1, 3, 2):
+        b = nrm.at[lax.rem(q + 4 - d, 4)]
+        remote(b, b, nm_s.at[d], nm_r.at[d], q_peer(d)).wait_recv()
+    norms_all = jnp.sqrt(((nrm[0] + nrm[1]) + (nrm[2] + nrm[3]))[0:1] + 1e-6)
     dpre_b, norms_b = make_dpre(1, dcode_b, pre_b)
     dpre_a, norms_a = make_dpre(0, dcode_a, pre_a)
 
@@ -586,8 +590,9 @@
             vmem((2, 128, 1024), f32),
             vmem((2, 128, 1024), bf16),
             vmem((2, 128, 1024), bf16),
-            vmem((4, 40, 256), f32), vmem((4, 40, 128), f32),
-            vmem((4, 40, 256), f32), vmem((4, 40, 128), f32),
+            vmem((4, 32, 256), bf16), vmem((4, 32, 128), bf16),
+            vmem((4, 32, 256), bf16), vmem((4, 32, 128), bf16),
+            vmem((4, 8, 384), f32),
             vmem((4, 32, 256), bf16), vmem((4, 32, 128), bf16),
             vmem((2, 12, 2, 16, 1024), bf16),
             vmem((3, 12, 16, 1024), bf16),
@@ -612,6 +617,7 @@
             dma((2, 4)), dma((2, 4)),
             dma((4,)), dma((4,)),
             dma((2, 4)), dma((2, 4)),
+            dma((4,)), dma((4,)),
             dma((2, 4)), dma((2, 4)),
             dma((3, 12)), dma((3, 12)),
             dma((12,)), dma((12,)),

time: 94.2 us -> 93.6 us (level)
  no operation moved by 1% of the time
where the time goes in v5:
time: 93.6 us; the launch traced here: 92.2 us
  Pallas kernels  88.2 us (94%)
  local copies, waits for them, and re-layouts  1.95 us (2%)
  other arithmetic  1.36 us (1%)
    pallas_call x1, Pallas kernels, step(): pl.pallas_call(kernel, out_shape=(jax.ShapeDtypeStruct((1, 8192), f32), j...  88.2 us

profile of v5, /device:TPU:1, one launch (start us, length us, event | category | flops | bytes accessed | tf_op | source)
XLA Modules:
  0.0 92.2 jit_solution(973968839283509794)
XLA Ops:
  0.6 0.0 copy-start.5
  0.6 0.0 copy-start.4
  0.7 0.0 copy-start
  0.7 0.8 copy-done
  1.4 0.0 copy-start.1
  1.4 0.7 copy-done.1
  2.1 0.0 copy-start.2
  2.1 0.0 copy-start.3
  2.1 88.2 %shard_map.126 = (f32[1,8192]{1,0:T(1,128)S(1)}, f32[8,128]{1,0:T(8,128)S(1)}) custom-call(bf16[128,8192]{1,0:T(8,128)(2,1)} %act.1, f32[1,8192]{1,0:T(1,128)S(1)} %copy-done, f32[1,96]{1,0:T(1,128)S(1)} %bitcast.9), custom_call_target="tpu_custom_call" | custom-call | tf_op jit(solution)/shard_map/pallas_call | solution.py:572
  90.3 0.5 slice.7
  90.8 0.0 copy-done.5
  90.8 0.0 copy-done.4
  90.8 0.5 divide_subtract_fusion.1
  91.4 0.0 copy-done.2
  91.4 0.0 copy-done.3
  91.4 0.8 divide_subtract_fusion
Async XLA Ops:
  0.6 90.2 %copy-start.5 = (f32[96]{0:T(128)S(1)}, f32[96]{0:T(128)}, u32[]{:S(2)}) copy-start(f32[96]{0:T(128)} %param.13) | copy-start | bytes 1156
  0.6 90.2 %copy-start.4 = (f32[96]{0:T(128)S(1)}, f32[96]{0:T(128)}, u32[]{:S(2)}) copy-start(f32[96]{0:T(128)} %param.12) | copy-start | bytes 1156
  0.7 0.8 copy-start
  1.4 0.7 copy-start.1
  2.1 89.3 %copy-start.2 = (f32[1,8192]{1,0:T(1,128)S(1)}, f32[1,8192]{1,0:T(1,128)}, u32[]{:S(2)}) copy-start(f32[1,8192]{1,0:T(1,128)} %param.9) | copy-start | bytes 98308
  2.1 89.3 %copy-start.3 = (f32[1,8192]{1,0:T(1,128)S(1)}, f32[1,8192]{1,0:T(1,128)}, u32[]{:S(2)}) copy-start(f32[1,8192]{1,0:T(1,128)} %param.10) | copy-start | bytes 98308
